TPU v7x, 32 devices: a whole 2x2x4 slice. The times are simulated.
32 devices in a mesh: team: 4 (over x, core), row: 8 (over z, y).
Axes of the slice: x: 2, y: 2, z: 4, core: 2. Of those that a mesh axis runs over, the one named last changes fastest.
Arguments:
- features: bfloat16 [16384, 128], P(('team', 'row')), may hold values from -6 to 6
- tile_values: bfloat16 [128, 12, 256, 256], P(('team', 'row')), may hold values from 0 to 0.09375, as said below
- tile_row: int32 [128, 12], P(('team', 'row')), may hold values from 0 to 1
- tile_col: int32 [128, 12], P(('team', 'row')), may hold values from 0 to 15
- tile_count: int32 [128], P(('team', 'row')), may hold values from 1 to 12, as said below
- weight: bfloat16 [128, 256], replicated, may hold values from -0.5 to 0.5
- bias: float32 [256], replicated, may hold values from -1.5 to 1.5
- cotangent: bfloat16 [16384, 256], P(('team', 'row')), may hold values from -0.046875 to 0.046875
Outputs:
- hidden: bfloat16 [16384, 256], P(('team', 'row'))
- weight_grad: float32 [128, 256], replicated
- bias_grad: float32 [256], replicated
Inputs may be any that keep to these rules, and one draw needn't show every extreme that they name: Live tiles stand in the first tile_count[g] slots of group g. In every draw some owner has 12 live tiles in each of its 4 groups. `tile_values`: every entry is a whole multiple of 1 / 32; most entries are zero.
All inputs are finite; a program needn't handle non-finite values.
Results may differ from a plain program's by a relative error of at most 0.0052.
Values may be sent and summed in bfloat16 or wider, within the bound.
A program may use at most 128 MiB of HBM per device.

v0:
```python
import jax
import jax.numpy as jnp
from jax import lax
from jax.sharding import PartitionSpec as P


def gelu_parts(values):
    gelu_coef = 0.7978845608
    tangent_h = jnp.tanh(gelu_coef * (values + 0.044715 * values * values * values))
    result = 0.5 * values * (1.0 + tangent_h)
    derive = 0.5 * (1.0 + tangent_h) + 0.5 * values * (1.0 - tangent_h * tangent_h) * gelu_coef * (
        1.0 + 3.0 * 0.044715 * values * values
    )
    return (result, derive)


def local(features, tile_values, tile_row, tile_col, tile_count, weight, bias, cotangent):
    team_count = lax.axis_size("team")
    block_size = tile_values.shape[2]
    slot_count = tile_values.shape[1]
    rows_dev = features.shape[0]
    in_width = features.shape[1]
    row_blocks = rows_dev // block_size
    slot_ids = jnp.arange(slot_count, dtype=jnp.int32)
    block_ids = jnp.arange(row_blocks, dtype=jnp.int32)
    total = jnp.zeros((row_blocks, block_size, in_width), jnp.float32)
    gathered = lax.all_gather(features, ("team", "row"), axis=0, tiled=True)
    panel_rows = gathered.shape[0] // team_count
    for panel_id in range(team_count):
        feature_panel = gathered[panel_id * panel_rows : (panel_id + 1) * panel_rows]
        panel_blocks = feature_panel.reshape(-1, block_size, in_width)
        tiles = lax.dynamic_index_in_dim(tile_values, panel_id, 0, False)
        row_index = lax.dynamic_index_in_dim(tile_row, panel_id, 0, False)
        col_index = lax.dynamic_index_in_dim(tile_col, panel_id, 0, False)
        count = lax.dynamic_index_in_dim(tile_count, panel_id, 0, False)
        picked = jnp.take(panel_blocks, col_index, axis=0)
        products = jnp.einsum("sij,sjf->sif", tiles, picked, preferred_element_type=jnp.float32)
        live_mask = slot_ids < count
        row_select = ((row_index[None, :] == block_ids[:, None]) & live_mask[None, :]).astype(
            jnp.float32
        )
        total = total + jnp.einsum(
            "rs,sif->rif", row_select, products, precision=lax.Precision.HIGHEST
        )
    aggregated = total.reshape(rows_dev, in_width).astype(jnp.bfloat16)
    pre = jnp.dot(aggregated, weight, preferred_element_type=jnp.float32) + bias
    result, derive = gelu_parts(pre)
    hidden = result.astype(jnp.bfloat16)
    slope = cotangent.astype(jnp.float32) * derive
    slope_half = slope.astype(jnp.bfloat16)
    weight_part = lax.dot_general(
        aggregated, slope_half, (((0,), (0,)), ((), ())), preferred_element_type=jnp.float32
    )
    bias_part = jnp.sum(slope, axis=0)
    summed = lax.psum((weight_part, bias_part), ("team", "row"))
    return (hidden, summed[0], summed[1])


def solution(mesh):
    in_specs = (
        P(("team", "row"), None),
        P(("team", "row"), None, None, None),
        P(("team", "row"), None),
        P(("team", "row"), None),
        P(("team", "row")),
        P(),
        P(),
        P(("team", "row"), None),
    )
    out_specs = (P(("team", "row"), None), P(), P())
    return jax.shard_map(local, mesh=mesh, in_specs=in_specs, out_specs=out_specs, check_vma=False)
```

profile of v0, /device:TPU:0, one launch (start us, length us, event | category | flops | bytes accessed | tf_op | source)
XLA Modules:
  0.0 248.4 jit_solution(145961915449625271)
XLA Ops:
  7.2 0.7 all-gather.2.cloned.1.call-update
  7.9 0.0 all-reduce.2.cloned.1.call-start
  8.0 1.4 fusion.83
  9.4 0.7 iota_compare_fusion
  10.0 0.7 iota_compare_fusion.2
  10.7 0.7 iota_compare_fusion.3
  11.3 0.6 iota_compare_fusion.1
  11.9 0.8 compare_and_fusion
  12.8 0.8 slice_bitcast_fusion
  13.6 62.3 %all-gather.2.cloned.1.call-done = bf16[16384,128]{1,0:T(8,128)(2,1)} async-done(((bf16[512,128]{1,0:T(8,128)(2,1)}), bf16[16384,128]{1,0:T(8,128)(2,1)}) %all-gather.2.cloned.1.call-update) | async-done | bytes 4194320 | tf_op jit(solution)/shard_map/all_gather | solution.py:27
  75.9 3.8 %fusion.82 = (bf16[4096,128]{1,0:T(8,128)(2,1)}, bf16[4096,128]{1,0:T(8,128)(2,1)S(1)}, bf16[4096,128]{1,0:T(8,128)(2,1)S(1)}, bf16[4096,128]{1,0:T(8,128)(2,1)}) fusion(bf16[16384,128]{1,0:T(8,128)(2,1)} %all-gather.2.cloned.1.call-done), kind=kLoop, calls=%fused_computation.101 | loop fusion | bytes 8388608 | tf_op jit(solution)/shard_map/slice | solution.py:30
  79.7 1.6 gather_fusion.1
  81.2 2.7 %fusion.12 = f32[12,128,256]{2,1,0:T(8,128)S(1)} fusion(bf16[4,12,256,256]{3,2,1,0:T(8,128)(2,1)} %param.11, bf16[12,256,128]{2,1,0:T(8,128)(2,1)} %gather_fusion.1, pred[12]{0:T(512)(128)(4,1)S(1)} %get-tuple-element.23), kind=kOutput, calls=%fused_computation.16 | convolution fusion | flops 201719808 | bytes 3932172 | tf_op jit(solution)/shard_map/sij,sjf->sif/dot_general | solution.py:37
  83.9 2.0 copy.13
  85.8 1.9 gather_fusion
  87.8 3.6 %fusion.14 = f32[12,128,256]{2,1,0:T(8,128)} fusion(bf16[4,12,256,256]{3,2,1,0:T(8,128)(2,1)} %param.11, bf16[12,256,128]{2,1,0:T(8,128)(2,1)S(1)} %gather_fusion, pred[12]{0:T(512)(128)(4,1)S(1)} %get-tuple-element.25), kind=kOutput, calls=%fused_computation.18 | convolution fusion | flops 201719808 | bytes 3932172 | tf_op jit(solution)/shard_map/sij,sjf->sif/dot_general | solution.py:37
  91.3 2.1 copy.12
  93.5 2.8 %gather_fusion.3 = bf16[12,256,128]{2,1,0:T(8,128)(2,1)} fusion(bf16[16,256,128]{2,1,0:T(8,128)(2,1)} %bitcast.78, s32[1024]{0:T(1024)S(1)} %get-tuple-element.33), kind=kCustom, calls=%fused_computation.3.clone | custom fusion | bytes 1572912 | tf_op jit(solution)/shard_map/jit(_take)/gather | solution.py:36
  96.3 3.8 %fusion.8 = f32[12,128,256]{2,1,0:T(8,128)} fusion(bf16[4,12,256,256]{3,2,1,0:T(8,128)(2,1)} %param.11, bf16[12,256,128]{2,1,0:T(8,128)(2,1)} %gather_fusion.3, pred[12]{0:T(512)(128)(4,1)S(1)} %get-tuple-element.6), kind=kOutput, calls=%fused_computation.12 | convolution fusion | flops 201719808 | bytes 3932172 | tf_op jit(solution)/shard_map/sij,sjf->sif/dot_general | solution.py:37
  100.1 2.9 %copy.15 = f32[12,128,256]{1,0,2:T(8,128)} copy(f32[12,128,256]{2,1,0:T(8,128)} %fusion.8) | data formatting | bytes 3145728 | tf_op jit(solution)/shard_map/sij,sjf->sif/dot_general | solution.py:37
  103.0 1.6 gather_fusion.2
  104.6 3.8 %fusion.10 = f32[12,128,256]{2,1,0:T(8,128)} fusion(bf16[4,12,256,256]{3,2,1,0:T(8,128)(2,1)} %param.11, bf16[12,256,128]{2,1,0:T(8,128)(2,1)} %gather_fusion.2, pred[12]{0:T(512)(128)(4,1)S(1)} %get-tuple-element.27), kind=kOutput, calls=%fused_computation.14 | convolution fusion | flops 201719808 | bytes 3932172 | tf_op jit(solution)/shard_map/sij,sjf->sif/dot_general | solution.py:37
  108.4 2.9 %copy.14 = f32[12,128,256]{1,0,2:T(8,128)} copy(f32[12,128,256]{2,1,0:T(8,128)} %fusion.10) | data formatting | bytes 3145728 | tf_op jit(solution)/shard_map/sij,sjf->sif/dot_general | solution.py:37
  111.4 2.5 %fusion.4 = f32[2,256,128]{2,0,1:T(2,128)S(1)} fusion(f32[12,128,256]{1,0,2:T(8,128)} %copy.13, pred[12]{0:T(512)(128)(4,1)S(1)} %iota_compare_fusion.2, s32[12]{0:T(128)S(1)} %get-tuple-element.20), kind=kOutput, calls=%fused_computation.8 | convolution fusion | flops 9437232 | bytes 1835068 | tf_op jit(solution)/shard_map/rs,sif->rif/dot_general | solution.py:42
  113.9 0.9 fusion.20
  114.8 0.9 fusion.23
  115.7 0.9 fusion.29
  116.6 1.3 fusion.80
  117.9 0.9 fusion.50
  118.8 39.2 %psum.15 = f32[256]{0:T(256)} all-reduce(f32[256]{0:T(256)S(1)} %get-tuple-element.4), channel_id=1, replica_groups=mesh['team'=4,'row'=8] {'team','row'}, use_global_device_ids=true, to_apply=%region_2.4 | all-reduce | flops 256 | bytes 2048 | tf_op jit(solution)/shard_map/psum | solution.py:55
  158.0 82.0 %all-reduce.2.cloned.1.call-done = f32[128,256]{1,0:T(8,128)} async-done(((f32[128,256]{1,0:T(8,128)}), f32[128,256]{1,0:T(8,128)}) %all-reduce.2.cloned.1.call-update) | async-done | bytes 131088 | tf_op jit(solution)/shard_map/psum | solution.py:55
  240.0 1.6 copy.17
  (15 shorter events, 0.1 us)
Async XLA Ops:
  7.2 109.5 %copy-start = (bf16[128,256]{1,0:T(8,128)(2,1)S(1)}, bf16[128,256]{1,0:T(8,128)(2,1)}, u32[]{:S(2)}) copy-start(bf16[128,256]{1,0:T(8,128)(2,1)} %param.15) | copy-start | bytes 196612
  7.2 68.7 %all-gather.2.cloned.1.call-start = ((), (), s32[]{:S(2)}) async-start(), calls=%async_computation | async-start | bytes 4325376 | tf_op jit(solution)/shard_map/all_gather | solution.py:27
  7.9 232.1 %all-reduce.2.cloned.1.call-start = ((), (), s32[]{:S(2)}) async-start(), calls=%async_computation.1 | async-start | bytes 262144 | tf_op jit(solution)/shard_map/psum | solution.py:55
  111.4 3.4 %copy-start.1 = (f32[12,128,256]{1,0,2:T(8,128)S(1)}, f32[12,128,256]{1,0,2:T(8,128)}, u32[]{:S(2)}) copy-start(f32[12,128,256]{1,0,2:T(8,128)} %copy.14) | copy-start | bytes 4718596
  113.9 1.8 copy-start.2
  114.8 1.8 copy-start.3
  114.8 1.8 copy-start.4
Sparse Core Ops, SparseCore 0:
  11.1 64.7 all-gather.1
  118.9 121.0 all-reduce.1
where the time goes:
time: 249 us; the launch traced here: 248 us
  waiting for transfers between devices  145 us (58%)
  blocking collectives  39.2 us (16%)
  local copies, waits for them, and re-layouts  25.4 us (10%)
  matrix products  21.2 us (9%)
  between operations  14.2 us (6%)
  other arithmetic  3.37 us (1%)
    psum x1, waiting for transfers between devices, local(): summed = lax.psum((weight_part, bias_part), ('team', 'row'))  82 us
    all_gather x1, waiting for transfers between devices, local(): gathered = lax.all_gather(features, ('team', 'row'), axis=0, tiled=True)  62.3 us
    psum x1, blocking collectives, local(): summed = lax.psum((weight_part, bias_part), ('team', 'row'))  39.2 us
    dot_general x4, matrix products, local(): jnp.einsum('sij,sjf->sif', tiles, picked, preferred_element_type=jnp.floa...  13.9 us
    dot_general x4, local copies, waits for them, and re-layouts, local(): jnp.einsum('sij,sjf->sif', tiles, picked, preferred_element_type=jnp.floa...  9.98 us
    gather x4, local copies, waits for them, and re-layouts, local(): picked = jnp.take(panel_blocks, col_index, axis=0)  7.81 us
    dot_general x4, matrix products, local(): jnp.einsum('rs,sif->rif', row_select, products, precision=lax.Precision.H...  5.15 us
  transfers between devices with their start and end apart: 2, of which 2 were waited for; matrix products, arithmetic and copies ran while one was open for 2% of the time, Pallas kernels for 0%

commit v1 on v0

v1 whole, which is shorter than its diff:
```python
import functools

import jax
import jax.numpy as jnp
from jax import lax
from jax.experimental import pallas as pl
from jax.experimental.pallas import tpu as pltpu
from jax.sharding import PartitionSpec as P

MESH = pl.DeviceIdType.MESH
GROUP = 16
LANES = 128


def gelu_parts(values):
    gelu_coef = 0.7978845608
    tangent_h = jnp.tanh(gelu_coef * (values + 0.044715 * values * values * values))
    result = 0.5 * values * (1.0 + tangent_h)
    derive = 0.5 * (1.0 + tangent_h) + 0.5 * values * (1.0 - tangent_h * tangent_h) * gelu_coef * (
        1.0 + 3.0 * 0.044715 * values * values
    )
    return (result, derive)


def flip(value, bits):
    result = value
    weight = 1
    while weight <= bits:
        if bits & weight:
            bit = lax.rem(lax.div(value, weight), 2)
            result = result + weight * (1 - 2 * bit)
        weight *= 2
    return result


def kernel(
    n_row,
    features,
    tile_values,
    tile_row,
    tile_col,
    tile_count,
    weight,
    bias,
    cotangent,
    hidden_out,
    weight_out,
    bias_out,
    near,
    near_other,
    far,
    far_other,
    tiles,
    weight_v,
    bias_v,
    cot_v,
    hidden_v,
    total,
    part,
    pair,
    red,
    scattered,
    bias_in,
    owned,
    crossed,
    fin,
    fin_other,
    local_sem,
    tile_sem,
    z_sem,
    x_sem,
    y_sem,
    xd_sem,
    yd_sem,
    core_sem,
    pair_sem,
    rs_sem,
    rb_sem,
    cross_sem,
    ag_sem,
    ab_sem,
):
    team, row = lax.axis_index("team"), lax.axis_index("row")
    a, core = lax.div(team, 2), lax.rem(team, 2)
    z, b = lax.div(row, 2), lax.rem(row, 2)
    n_z = n_row // 2
    slots = tile_values.shape[1]
    blk = tile_values.shape[2]

    x_dev = ((1 - a) * 2 + core, row)
    y_dev = (team, z * 2 + (1 - b))
    c_dev = (a * 2 + (1 - core), row)

    def rows_of(z_now, b_now):
        return pl.ds(2 * (z_now * 2 + b_now), 2)

    own = rows_of(z, b)
    load_own = pltpu.make_async_copy(features, near.at[own], local_sem.at[0])
    load_own.start()
    panels = [a * 2 + core, a * 2 + 1 - core, (1 - a) * 2 + core, (1 - a) * 2 + 1 - core]
    loads = [
        pltpu.make_async_copy(weight, weight_v, local_sem.at[1]),
        pltpu.make_async_copy(bias, bias_v, local_sem.at[2]),
        pltpu.make_async_copy(cotangent, cot_v, local_sem.at[3]),
    ]
    tile_loads = [
        pltpu.make_async_copy(tile_values.at[panel], tiles.at[i], tile_sem.at[i])
        for i, panel in enumerate(panels)
    ]

    barrier = pltpu.get_barrier_semaphore()
    greeted = [c_dev]
    for i in range(1, 2 * n_row):
        flat = lax.rem(a * n_row + row + i, 2 * n_row)
        greeted.append((lax.div(flat, n_row) * 2 + core, lax.rem(flat, n_row)))
    for dev in greeted:
        pl.semaphore_signal(barrier, inc=1, device_id=dev, device_id_type=MESH)
    for copy in tile_loads + loads:
        copy.start()
    pl.semaphore_wait(barrier, len(greeted))
    load_own.wait()

    sent = []

    def remote(src, dst, sems, i, dev):
        return pltpu.make_async_remote_copy(
            src_ref=src,
            dst_ref=dst,
            send_sem=sems.at[0, i],
            recv_sem=sems.at[1, i],
            device_id=dev,
            device_id_type=MESH,
        )

    def send(src, dst, sems, i, dev):
        copy = remote(src, dst, sems, i, dev)
        copy.start()
        sent.append(copy)

    def arrived(ref, sems, i, dev):
        remote(ref, ref, sems, i, dev).wait_recv()

    def full(j):
        z_now = flip(z, j)
        rows = rows_of(z_now, b)
        if j > 0:
            arrived(near.at[rows], z_sem, j, (team, z_now * 2 + b))
        send(near.at[rows], near.at[rows], y_sem, j, y_dev)
        send(near.at[rows], far.at[rows], x_sem, j, x_dev)
        if j == 0:
            for k in range(1, n_z):
                dev = (team, flip(z, k) * 2 + b)
                send(near.at[rows], near.at[rows], z_sem, k, dev)
        send(near.at[rows], near_other.at[rows], core_sem, j, c_dev)

    def diagonal(j):
        z_now = flip(z, j)
        mine, other = rows_of(z_now, b), rows_of(z_now, 1 - b)
        arrived(near.at[other], y_sem, j, y_dev)
        second = 2 * (z_now * 2 + 1 - b) + 1
        send(near.at[second], far.at[second], xd_sem, j, x_dev)
        send(near.at[other], near_other.at[other], core_sem, n_z + j, c_dev)
        arrived(far.at[mine], x_sem, j, x_dev)
        first = 2 * (z_now * 2 + b)
        send(far.at[first], far.at[first], yd_sem, j, y_dev)
        send(far.at[mine], far_other.at[mine], core_sem, 2 * n_z + j, c_dev)

    def last(j):
        other = rows_of(flip(z, j), 1 - b)
        first = 2 * (flip(z, j) * 2 + 1 - b)
        arrived(far.at[first + 1], xd_sem, j, x_dev)
        arrived(far.at[first], yd_sem, j, y_dev)
        send(far.at[other], far_other.at[other], core_sem, 3 * n_z + j, c_dev)

    def from_core(ref, first, b_now):
        for j in range(n_z):
            rows = rows_of(flip(z, j), b_now)
            arrived(ref.at[rows], core_sem, first * n_z + j, c_dev)

    def aggregate(i, feats):
        tile_loads[i].wait()
        panel = panels[i]
        count = tile_count[panel]
        step = 6 if slots % 6 == 0 else slots
        for base in range(0, slots, step):
            left, right = [], []
            for s in range(base, base + step):
                block = feats[tile_col[panel, s]]
                live = s < count
                place = tile_row[panel, s]
                zero = jnp.zeros_like(block)
                upper = jnp.where(live & (place == 0), block, zero)
                lower = jnp.where(live & (place == 1), block, zero)
                left.append(tiles[i, s])
                right.append(jnp.concatenate([upper, lower], axis=1))
            product = jnp.dot(
                jnp.concatenate(left, axis=1),
                jnp.concatenate(right, axis=0),
                preferred_element_type=jnp.float32,
            )
            if i == 0 and base == 0:
                total[...] = product
            else:
                total[...] += product

    full(0)
    for j in range(1, n_z):
        full(j)
        diagonal(j - 1)
    diagonal(n_z - 1)
    aggregate(0, near)
    for j in range(n_z // 2):
        last(j)
    from_core(near_other, 0, b)
    from_core(near_other, 1, 1 - b)
    aggregate(1, near_other)
    for j in range(n_z // 2, n_z):
        last(j)
    aggregate(2, far)
    from_core(far_other, 2, b)
    from_core(far_other, 3, 1 - b)
    aggregate(3, far_other)

    for copy in loads:
        copy.wait()
    step = 128
    weight_part = jnp.zeros((weight_v.shape[0], weight_v.shape[1]), jnp.float32)
    bias_part = jnp.zeros((1, weight_v.shape[1]), jnp.float32)
    for r in range(0, 2 * blk, step):
        lane = (r // blk) * LANES
        inner = r % blk
        agg = total[inner : inner + step, lane : lane + LANES].astype(jnp.bfloat16)
        pre = jnp.dot(agg, weight_v[...], preferred_element_type=jnp.float32) + bias_v[...]
        result, derive = gelu_parts(pre)
        hidden_v[r : r + step, :] = result.astype(jnp.bfloat16)
        slope = cot_v[r : r + step, :].astype(jnp.float32) * derive
        weight_part = weight_part + lax.dot_general(
            agg,
            slope.astype(jnp.bfloat16),
            (((0,), (0,)), ((), ())),
            preferred_element_type=jnp.float32,
        )
        bias_part = bias_part + jnp.sum(slope, axis=0, keepdims=True)
    for h in range(2):
        lanes = slice(h * LANES, (h + 1) * LANES)
        part[h, 0:GROUP] = weight_part[:, lanes].reshape(GROUP, 8, LANES)
        part[h, GROUP] = jnp.broadcast_to(bias_part[:, lanes], (8, LANES))
    store_hidden = pltpu.make_async_copy(hidden_v, hidden_out, local_sem.at[0])
    store_hidden.start()

    send(part.at[1 - core], pair, pair_sem, 0, c_dev)
    arrived(pair, pair_sem, 0, c_dev)
    red[...] = part[core] + pair[...]

    group, member = lax.div(row, 8), a * 8 + lax.rem(row, 8)

    def at(member_now, group_now):
        return (lax.div(member_now, 8) * 2 + core, group_now * 8 + lax.rem(member_now, 8))

    head = at(0, group)
    for i in range(1, GROUP):
        peer = lax.rem(member + i, GROUP)
        send(red.at[peer], scattered.at[member], rs_sem, i, at(peer, group))

    @pl.when(member != 0)
    def _():
        copy = pltpu.make_async_remote_copy(
            src_ref=red.at[GROUP],
            dst_ref=bias_in.at[member],
            send_sem=rb_sem.at[0, 0],
            recv_sem=rb_sem.at[1, member],
            device_id=head,
            device_id_type=MESH,
        )
        copy.start()
        copy.wait_send()

    scattered[member] = red[member]
    owned[1] = jnp.zeros((8, LANES), jnp.float32)
    for i in range(1, GROUP):
        peer = lax.rem(member + GROUP - i, GROUP)
        arrived(scattered.at[peer], rs_sem, i, at(peer, group))
    owned[0] = jnp.sum(scattered[...], axis=0)

    @pl.when(member == 0)
    def _():
        bias_in[0] = red[GROUP]
        for i in range(1, GROUP):
            remote(bias_in.at[i], bias_in.at[i], rb_sem, i, c_dev).wait_recv()
        owned[1] = jnp.sum(bias_in[...], axis=0)

    n_group = n_row // 8
    if n_group > 1:
        for g in range(1, n_group):
            dev = at(member, lax.rem(group + g, n_group))
            send(owned, crossed.at[g], cross_sem, g, dev)
        crossed[0] = owned[...]
        for g in range(1, n_group):
            arrived(crossed.at[g], cross_sem, g, at(member, lax.rem(group + n_group - g, n_group)))
        for g in range(1, n_group):
            sent.pop().wait_send()
        ordered = jnp.zeros(owned.shape, jnp.float32)
        for g in range(n_group):
            ordered = ordered + crossed[lax.rem(group + n_group - g, n_group)]
        owned[...] = ordered

    for i in range(1, GROUP):
        peer = lax.rem(member + i, GROUP)
        send(owned.at[0], fin.at[member], ag_sem, i, at(peer, group))

    @pl.when(member == 0)
    def _():
        copies = [
            remote(owned.at[1], fin.at[GROUP], ab_sem, i, at(i, group)) for i in range(1, GROUP)
        ]
        for copy in copies:
            copy.start()
        fin[GROUP] = owned[1]
        for copy in copies:
            copy.wait_send()

    @pl.when(member != 0)
    def _():
        pltpu.make_async_remote_copy(
            src_ref=owned.at[1],
            dst_ref=fin.at[GROUP],
            send_sem=ab_sem.at[0, 0],
            recv_sem=ab_sem.at[1, member],
            device_id=head,
            device_id_type=MESH,
        ).wait_recv()

    fin[member] = owned[0]
    for i in range(1, GROUP):
        peer = lax.rem(member + GROUP - i, GROUP)
        arrived(fin.at[peer], ag_sem, i, at(peer, group))
    send(fin, fin_other, pair_sem, 1, c_dev)
    arrived(fin_other, pair_sem, 1, c_dev)
    mine, other = fin[...], fin_other[...]
    for h in range(2):
        half = jnp.where(core == h, mine, other)
        lanes = slice(h * LANES, (h + 1) * LANES)
        weight_out[:, lanes] = half[0:GROUP].reshape(GROUP * 8, LANES)
        bias_out[:, lanes] = half[GROUP, 0:1]
    for copy in sent:
        copy.wait_send()
    store_hidden.wait()


def local(n_row, features, tile_values, tile_row, tile_col, tile_count, weight, bias, cotangent):
    n_panel, slots, blk, _ = tile_values.shape
    rows, width = features.shape
    wide = weight.shape[1]
    n_z = n_row // 2
    n_group = n_row // 8
    dma = pltpu.SemaphoreType.DMA
    anywhere = pl.BlockSpec(memory_space=pl.ANY)
    smem = pl.BlockSpec(memory_space=pltpu.SMEM)
    vmem = pl.BlockSpec(memory_space=pltpu.VMEM)
    hidden, weight_grad, bias_grad = pl.pallas_call(
        functools.partial(kernel, n_row),
        out_shape=[
            jax.ShapeDtypeStruct((rows, wide), jnp.bfloat16),
            jax.ShapeDtypeStruct((width, wide), jnp.float32),
            jax.ShapeDtypeStruct((1, wide), jnp.float32),
        ],
        in_specs=[anywhere, anywhere, smem, smem, smem, anywhere, anywhere, anywhere],
        out_specs=[anywhere, vmem, vmem],
        scratch_shapes=[
            pltpu.VMEM((2 * n_row, blk, width), jnp.bfloat16),
            pltpu.VMEM((2 * n_row, blk, width), jnp.bfloat16),
            pltpu.VMEM((2 * n_row, blk, width), jnp.bfloat16),
            pltpu.VMEM((2 * n_row, blk, width), jnp.bfloat16),
            pltpu.VMEM((n_panel, slots, blk, blk), jnp.bfloat16),
            pltpu.VMEM((width, wide), jnp.bfloat16),
            pltpu.VMEM((1, wide), jnp.float32),
            pltpu.VMEM((rows, wide), jnp.bfloat16),
            pltpu.VMEM((rows, wide), jnp.bfloat16),
            pltpu.VMEM((blk, 2 * width), jnp.float32),
            pltpu.VMEM((2, GROUP + 1, 8, LANES), jnp.float32),
            pltpu.VMEM((GROUP + 1, 8, LANES), jnp.float32),
            pltpu.VMEM((GROUP + 1, 8, LANES), jnp.float32),
            pltpu.VMEM((GROUP, 8, LANES), jnp.float32),
            pltpu.VMEM((GROUP, 8, LANES), jnp.float32),
            pltpu.VMEM((2, 8, LANES), jnp.float32),
            pltpu.VMEM((n_group, 2, 8, LANES), jnp.float32),
            pltpu.VMEM((GROUP + 1, 8, LANES), jnp.float32),
            pltpu.VMEM((GROUP + 1, 8, LANES), jnp.float32),
            dma((4,)),
            dma((4,)),
            dma((2, n_z)),
            dma((2, n_z)),
            dma((2, n_z)),
            dma((2, n_z)),
            dma((2, n_z)),
            dma((2, 4 * n_z)),
            dma((2, 2)),
            dma((2, GROUP)),
            dma((2, GROUP)),
            dma((2, n_group)),
            dma((2, GROUP)),
            dma((2, GROUP)),
        ],
        compiler_params=pltpu.CompilerParams(
            collective_id=0, has_side_effects=True, vmem_limit_bytes=56 * 1024 * 1024
        ),
    )(
        features.reshape(rows // blk, blk, width),
        tile_values,
        tile_row,
        tile_col,
        tile_count,
        weight,
        bias.reshape(1, wide),
        cotangent,
    )
    return (hidden, weight_grad, bias_grad.reshape(wide))


def solution(mesh):
    in_specs = (
        P(("team", "row"), None),
        P(("team", "row"), None, None, None),
        P(("team", "row"), None),
        P(("team", "row"), None),
        P(("team", "row")),
        P(),
        P(),
        P(("team", "row"), None),
    )
    out_specs = (P(("team", "row"), None), P(), P())
    return jax.shard_map(
        functools.partial(local, mesh.shape["row"]),
        mesh=mesh,
        in_specs=in_specs,
        out_specs=out_specs,
        check_vma=False,
    )
```

time: 249 us -> 53.5 us (0.21)
  waiting for transfers between devices: 145 us -> 0 us
  Pallas kernels: 0 us -> 48.2 us
  blocking collectives: 39.2 us -> 0 us
  matrix products: 21.2 us -> 0 us
  local copies, waits for them, and re-layouts: 25.4 us -> 4.43 us
  between operations: 14.2 us -> 0.64 us
  other arithmetic: 3.37 us -> 0 us
    psum x1 -> x0, waiting for transfers between devices: 82 us -> none  [local(): summed = lax.psum((weight_part, bias_part), ('team', 'row'))]
    all_gather x1 -> x0, waiting for transfers between devices: 62.3 us -> none  [local(): gathered = lax.all_gather(features, ('team', 'row'), axis=0, tiled=True)]
    pallas_call x0 -> x1, Pallas kernels: none -> 48.2 us  [local(): pl.pallas_call(functools.partial(kernel, n_row), out_shape=[jax.ShapeDtyp...]
    psum x1 -> x0, blocking collectives: 39.2 us -> none  [local(): summed = lax.psum((weight_part, bias_part), ('team', 'row'))]
    dot_general x10 -> x0, matrix products: 21.2 us -> none  [the longest x4 13.9 us: local(): jnp.einsum('sij,sjf->sif', tiles, picked, preferred_element_type=jnp.floa...]
    dot_general x4 -> x0, local copies, waits for them, and re-layouts: 9.98 us -> none  [local(): jnp.einsum('sij,sjf->sif', tiles, picked, preferred_element_type=jnp.floa...]
    gather x4 -> x0, local copies, waits for them, and re-layouts: 7.81 us -> none  [local(): picked = jnp.take(panel_blocks, col_index, axis=0)]
    slice x1 -> x0, local copies, waits for them, and re-layouts: 3.76 us -> none  [local(): feature_panel = gathered[panel_id * panel_rows:(panel_id + 1) * panel_rows]]
  transfers between devices with their start and end apart: 2 -> 0, of which waited for: 2 -> 0; matrix products, arithmetic and copies ran while one was open for 2% -> 0% of each run, Pallas kernels for 0% -> 0%
where the time goes in v1:
time: 53.5 us; the launch traced here: 53.3 us
  Pallas kernels  48.2 us (90%)
  local copies, waits for them, and re-layouts  4.43 us (8%)
  between operations  0.64 us (1%)
    pallas_call x1, Pallas kernels, local(): pl.pallas_call(functools.partial(kernel, n_row), out_shape=[jax.ShapeDtyp...  48.2 us
    unnamed x3, local copies, waits for them, and re-layouts  4.43 us

profile of v1, /device:TPU:0, one launch (start us, length us, event | category | flops | bytes accessed | tf_op | source)
XLA Modules:
  0.0 53.3 jit_solution(17248562097581724424)
XLA Ops:
  0.6 48.2 %shard_map.103 = (bf16[512,256]{1,0:T(8,128)(2,1)}, f32[128,256]{1,0:T(8,128)}, f32[1,256]{1,0:T(1,128)}) custom-call(bf16[2,256,128]{2,1,0:T(8,128)(2,1)} %bitcast.3, bf16[4,12,256,256]{3,2,1,0:T(8,128)(2,1)} %tile_values.1, s32[4,12]{1,0:T(4,128)} %tile_row.1, s32[4,12]{1,0:T(4,128)} %tile_col.1, s32[4]{0:T(128)} %tile_count.1, bf16[128,256]{1,0:T(8,128)(2,1)} %weight.1, ...), custom_call_target="tpu_custom_call" | custom-call | tf_op jit(solution)/shard_map/pallas_call | solution.py:360
  48.8 1.7 %copy.14 = bf16[512,256]{1,0:T(8,128)(2,1)} copy(bf16[512,256]{1,0:T(8,128)(2,1)} %get-tuple-element.12) | data formatting | bytes 524288
  50.5 1.6 %copy.15 = f32[128,256]{1,0:T(8,128)} copy(f32[128,256]{1,0:T(8,128)} %get-tuple-element.13) | data formatting | bytes 262144
  52.1 1.2 %copy.16 = f32[256]{0:T(256)} copy(f32[256]{0:T(256)} %bitcast.4) | data formatting | bytes 2048

commit v2 on v1

--- a/solution.py
+++ b/solution.py
@@ -65,6 +65,8 @@
     crossed,
     fin,
     fin_other,
+    wg,
+    bg,
     local_sem,
     tile_sem,
     z_sem,
@@ -135,56 +137,95 @@
     def send(src, dst, sems, i, dev):
         copy = remote(src, dst, sems, i, dev)
         copy.start()
-        sent.append(copy)
+        return copy
 
     def arrived(ref, sems, i, dev):
         remote(ref, ref, sems, i, dev).wait_recv()
 
-    def full(j):
-        z_now = flip(z, j)
-        rows = rows_of(z_now, b)
-        if j > 0:
-            arrived(near.at[rows], z_sem, j, (team, z_now * 2 + b))
-        send(near.at[rows], near.at[rows], y_sem, j, y_dev)
-        send(near.at[rows], far.at[rows], x_sem, j, x_dev)
-        if j == 0:
-            for k in range(1, n_z):
-                dev = (team, flip(z, k) * 2 + b)
-                send(near.at[rows], near.at[rows], z_sem, k, dev)
-        send(near.at[rows], near_other.at[rows], core_sem, j, c_dev)
-
-    def diagonal(j):
-        z_now = flip(z, j)
-        mine, other = rows_of(z_now, b), rows_of(z_now, 1 - b)
-        arrived(near.at[other], y_sem, j, y_dev)
-        second = 2 * (z_now * 2 + 1 - b) + 1
-        send(near.at[second], far.at[second], xd_sem, j, x_dev)
-        send(near.at[other], near_other.at[other], core_sem, n_z + j, c_dev)
-        arrived(far.at[mine], x_sem, j, x_dev)
-        first = 2 * (z_now * 2 + b)
-        send(far.at[first], far.at[first], yd_sem, j, y_dev)
-        send(far.at[mine], far_other.at[mine], core_sem, 2 * n_z + j, c_dev)
-
-    def last(j):
-        other = rows_of(flip(z, j), 1 - b)
-        first = 2 * (flip(z, j) * 2 + 1 - b)
-        arrived(far.at[first + 1], xd_sem, j, x_dev)
-        arrived(far.at[first], yd_sem, j, y_dev)
-        send(far.at[other], far_other.at[other], core_sem, 3 * n_z + j, c_dev)
+    def full(source):
+        rows = rows_of(source, b)
+        send(near.at[rows], near.at[rows], y_sem, source, y_dev)
+        send(near.at[rows], far.at[rows], x_sem, source, x_dev)
+        send(near.at[rows], near_other.at[rows], core_sem, source, c_dev)
+
+    def pass_on(source, way):
+        rows = rows_of(source, b)
+        dev = (team, (z + 1 - 2 * way) * 2 + b)
+
+        def copy():
+            return remote(near.at[rows], near.at[rows], z_sem, way * n_z + source, dev)
+
+        @pl.when(z < n_z - 1 if way == 0 else z > 0)
+        def _():
+            copy().start()
+
+    def diagonal(source):
+        mine, other = rows_of(source, b), rows_of(source, 1 - b)
+        arrived(near.at[other], y_sem, source, y_dev)
+        second = 2 * (source * 2 + 1 - b) + 1
+        send(near.at[second], far.at[second], xd_sem, source, x_dev)
+        send(near.at[other], near_other.at[other], core_sem, n_z + source, c_dev)
+        arrived(far.at[mine], x_sem, source, x_dev)
+        first = 2 * (source * 2 + b)
+        send(far.at[first], far.at[first], yd_sem, source, y_dev)
+        send(far.at[mine], far_other.at[mine], core_sem, 2 * n_z + source, c_dev)
+
+    def last(source):
+        other = rows_of(source, 1 - b)
+        first = 2 * (source * 2 + 1 - b)
+        arrived(far.at[first + 1], xd_sem, source, x_dev)
+        arrived(far.at[first], yd_sem, source, y_dev)
+        send(far.at[other], far_other.at[other], core_sem, 3 * n_z + source, c_dev)
+
+    def both_ways(t, act):
+        for way in range(2):
+            source = z - t if way == 0 else z + t
+
+            @pl.when(source >= 0 if way == 0 else source < n_z)
+            def _():
+                act(source, way)
+
+    def receive(source, way):
+        rows = rows_of(source, b)
+        dev = (team, (z - 1 + 2 * way) * 2 + b)
+        arrived(near.at[rows], z_sem, way * n_z + source, dev)
+        pass_on(source, way)
+        full(source)
 
     def from_core(ref, first, b_now):
         for j in range(n_z):
-            rows = rows_of(flip(z, j), b_now)
-            arrived(ref.at[rows], core_sem, first * n_z + j, c_dev)
+            arrived(ref.at[rows_of(j, b_now)], core_sem, first * n_z + j, c_dev)
+
+    def all_sent():
+        for way in range(2):
+            for source in range(n_z):
+                goes = (z < n_z - 1) & (z >= source) if way == 0 else (z > 0) & (z <= source)
+                rows = rows_of(source, b)
+
+                @pl.when(goes)
+                def _():
+                    remote(near.at[rows], near.at[rows], z_sem, way * n_z + source, c_dev).wait_send()
+
+        for source in range(n_z):
+            rows = rows_of(source, b)
+            for sems in (y_sem, x_sem):
+                remote(near.at[rows], near.at[rows], sems, source, c_dev).wait_send()
+            for sems in (xd_sem, yd_sem):
+                one = near.at[2 * source]
+                remote(one, one, sems, source, c_dev).wait_send()
+            for kind in range(4):
+                remote(near.at[rows], near.at[rows], core_sem, kind * n_z + source, c_dev).wait_send()
 
     def aggregate(i, feats):
         tile_loads[i].wait()
         panel = panels[i]
         count = tile_count[panel]
-        step = 6 if slots % 6 == 0 else slots
-        for base in range(0, slots, step):
+        step = 4 if slots % 4 == 0 else slots
+
+        def add(base, carry):
             left, right = [], []
-            for s in range(base, base + step):
+            for k in range(step):
+                s = base * step + k
                 block = feats[tile_col[panel, s]]
                 live = s < count
                 place = tile_row[panel, s]
@@ -193,29 +234,37 @@
                 lower = jnp.where(live & (place == 1), block, zero)
                 left.append(tiles[i, s])
                 right.append(jnp.concatenate([upper, lower], axis=1))
-            product = jnp.dot(
+            total[...] += jnp.dot(
                 jnp.concatenate(left, axis=1),
                 jnp.concatenate(right, axis=0),
                 preferred_element_type=jnp.float32,
             )
-            if i == 0 and base == 0:
-                total[...] = product
-            else:
-                total[...] += product
-
-    full(0)
-    for j in range(1, n_z):
-        full(j)
-        diagonal(j - 1)
-    diagonal(n_z - 1)
+            return carry
+
+        lax.fori_loop(0, slots // step, add, 0)
+
+    pass_on(z, 0)
+    pass_on(z, 1)
+    full(z)
+    total[...] = jnp.zeros_like(total)
+    wg[...] = jnp.zeros_like(wg)
+    bg[...] = jnp.zeros_like(bg)
+    for t in range(1, n_z):
+        both_ways(t, receive)
+        if t == 1:
+            diagonal(z)
+        else:
+            both_ways(t - 1, lambda source, way: diagonal(source))
+    both_ways(n_z - 1, lambda source, way: diagonal(source))
     aggregate(0, near)
-    for j in range(n_z // 2):
-        last(j)
+    last(z)
+    for t in range(1, n_z // 2):
+        both_ways(t, lambda source, way: last(source))
     from_core(near_other, 0, b)
     from_core(near_other, 1, 1 - b)
     aggregate(1, near_other)
-    for j in range(n_z // 2, n_z):
-        last(j)
+    for t in range(n_z // 2, n_z):
+        both_ways(t, lambda source, way: last(source))
     aggregate(2, far)
     from_core(far_other, 2, b)
     from_core(far_other, 3, 1 - b)
@@ -224,23 +273,27 @@
     for copy in loads:
         copy.wait()
     step = 128
-    weight_part = jnp.zeros((weight_v.shape[0], weight_v.shape[1]), jnp.float32)
-    bias_part = jnp.zeros((1, weight_v.shape[1]), jnp.float32)
-    for r in range(0, 2 * blk, step):
-        lane = (r // blk) * LANES
-        inner = r % blk
-        agg = total[inner : inner + step, lane : lane + LANES].astype(jnp.bfloat16)
-        pre = jnp.dot(agg, weight_v[...], preferred_element_type=jnp.float32) + bias_v[...]
-        result, derive = gelu_parts(pre)
-        hidden_v[r : r + step, :] = result.astype(jnp.bfloat16)
-        slope = cot_v[r : r + step, :].astype(jnp.float32) * derive
-        weight_part = weight_part + lax.dot_general(
-            agg,
-            slope.astype(jnp.bfloat16),
-            (((0,), (0,)), ((), ())),
-            preferred_element_type=jnp.float32,
-        )
-        bias_part = bias_part + jnp.sum(slope, axis=0, keepdims=True)
+    for h in range(2):
+
+        def layer(k, carry):
+            inner = pl.ds(pl.multiple_of(k * step, step), step)
+            outer = pl.ds(pl.multiple_of(h * blk + k * step, step), step)
+            agg = total[inner, h * LANES : (h + 1) * LANES].astype(jnp.bfloat16)
+            pre = jnp.dot(agg, weight_v[...], preferred_element_type=jnp.float32) + bias_v[...]
+            result, derive = gelu_parts(pre)
+            hidden_v[outer, :] = result.astype(jnp.bfloat16)
+            slope = cot_v[outer, :].astype(jnp.float32) * derive
+            wg[...] += lax.dot_general(
+                agg,
+                slope.astype(jnp.bfloat16),
+                (((0,), (0,)), ((), ())),
+                preferred_element_type=jnp.float32,
+            )
+            bg[...] += jnp.sum(slope, axis=0, keepdims=True)
+            return carry
+
+        lax.fori_loop(0, blk // step, layer, 0)
+    weight_part, bias_part = wg[...], bg[...]
     for h in range(2):
         lanes = slice(h * LANES, (h + 1) * LANES)
         part[h, 0:GROUP] = weight_part[:, lanes].reshape(GROUP, 8, LANES)
@@ -248,7 +301,7 @@
     store_hidden = pltpu.make_async_copy(hidden_v, hidden_out, local_sem.at[0])
     store_hidden.start()
 
-    send(part.at[1 - core], pair, pair_sem, 0, c_dev)
+    sent.append(send(part.at[1 - core], pair, pair_sem, 0, c_dev))
     arrived(pair, pair_sem, 0, c_dev)
     red[...] = part[core] + pair[...]
 
@@ -260,7 +313,7 @@
     head = at(0, group)
     for i in range(1, GROUP):
         peer = lax.rem(member + i, GROUP)
-        send(red.at[peer], scattered.at[member], rs_sem, i, at(peer, group))
+        sent.append(send(red.at[peer], scattered.at[member], rs_sem, i, at(peer, group)))
 
     @pl.when(member != 0)
     def _():
@@ -293,7 +346,7 @@
     if n_group > 1:
         for g in range(1, n_group):
             dev = at(member, lax.rem(group + g, n_group))
-            send(owned, crossed.at[g], cross_sem, g, dev)
+            sent.append(send(owned, crossed.at[g], cross_sem, g, dev))
         crossed[0] = owned[...]
         for g in range(1, n_group):
             arrived(crossed.at[g], cross_sem, g, at(member, lax.rem(group + n_group - g, n_group)))
@@ -306,7 +359,7 @@
 
     for i in range(1, GROUP):
         peer = lax.rem(member + i, GROUP)
-        send(owned.at[0], fin.at[member], ag_sem, i, at(peer, group))
+        sent.append(send(owned.at[0], fin.at[member], ag_sem, i, at(peer, group)))
 
     @pl.when(member == 0)
     def _():
@@ -334,7 +387,7 @@
     for i in range(1, GROUP):
         peer = lax.rem(member + GROUP - i, GROUP)
         arrived(fin.at[peer], ag_sem, i, at(peer, group))
-    send(fin, fin_other, pair_sem, 1, c_dev)
+    sent.append(send(fin, fin_other, pair_sem, 1, c_dev))
     arrived(fin_other, pair_sem, 1, c_dev)
     mine, other = fin[...], fin_other[...]
     for h in range(2):
@@ -344,7 +397,20 @@
         bias_out[:, lanes] = half[GROUP, 0:1]
     for copy in sent:
         copy.wait_send()
+    all_sent()
     store_hidden.wait()
+
+
+def hand_over(hidden, weight_grad, bias_grad, hidden_out, weight_out, bias_out, sems):
+    copies = [
+        pltpu.make_async_copy(hidden, hidden_out, sems.at[0]),
+        pltpu.make_async_copy(weight_grad, weight_out, sems.at[1]),
+        pltpu.make_async_copy(bias_grad, bias_out, sems.at[2]),
+    ]
+    for copy in copies:
+        copy.start()
+    for copy in copies:
+        copy.wait()
 
 
 def local(n_row, features, tile_values, tile_row, tile_col, tile_count, weight, bias, cotangent):
@@ -386,9 +452,11 @@
             pltpu.VMEM((n_group, 2, 8, LANES), jnp.float32),
             pltpu.VMEM((GROUP + 1, 8, LANES), jnp.float32),
             pltpu.VMEM((GROUP + 1, 8, LANES), jnp.float32),
+            pltpu.VMEM((width, wide), jnp.float32),
+            pltpu.VMEM((1, wide), jnp.float32),
             dma((4,)),
             dma((4,)),
-            dma((2, n_z)),
+            dma((2, 2 * n_z)),
             dma((2, n_z)),
             dma((2, n_z)),
             dma((2, n_z)),
@@ -414,6 +482,15 @@
         bias.reshape(1, wide),
         cotangent,
     )
+    shapes = [jax.ShapeDtypeStruct(x.shape, x.dtype) for x in (hidden, weight_grad, bias_grad)]
+    hidden, weight_grad, bias_grad = pl.pallas_call(
+        hand_over,
+        out_shape=shapes,
+        in_specs=[anywhere] * 3,
+        out_specs=[anywhere] * 3,
+        scratch_shapes=[dma((3,))],
+        compiler_params=pltpu.CompilerParams(vmem_limit_bytes=60 * 1024 * 1024),
+    )(hidden, weight_grad, bias_grad)
     return (hidden, weight_grad, bias_grad.reshape(wide))
 
 

time: 53.5 us -> 60 us (1.12)
  Pallas kernels: 48.2 us -> 59.2 us
  local copies, waits for them, and re-layouts: 4.43 us -> 0 us
    pallas_call x0 -> x1, Pallas kernels: none -> 13.1 us  [local(): pl.pallas_call(hand_over, out_shape=shapes, in_specs=[anywhere] * 3, out_...]
    unnamed x3 -> x0, local copies, waits for them, and re-layouts: 4.43 us -> none
    pallas_call x1, Pallas kernels: 48.2 us -> 46.1 us  [local(): pl.pallas_call(functools.partial(kernel, n_row), out_shape=[jax.ShapeDtyp...]
where the time goes in v2:
time: 60 us; the launch traced here: 59.8 us
  Pallas kernels  59.2 us (99%)
  between operations  0.64 us (1%)
    pallas_call x1, Pallas kernels, local(): pl.pallas_call(functools.partial(kernel, n_row), out_shape=[jax.ShapeDtyp...  46.1 us
    pallas_call x1, Pallas kernels, local(): pl.pallas_call(hand_over, out_shape=shapes, in_specs=[anywhere] * 3, out_...  13.1 us

profile of v2, /device:TPU:0, one launch (start us, length us, event | category | flops | bytes accessed | tf_op | source)
XLA Modules:
  0.0 59.8 jit_solution(11587550041939941503)
XLA Ops:
  0.6 46.1 %shard_map.103 = (bf16[512,256]{1,0:T(8,128)(2,1)}, f32[128,256]{1,0:T(8,128)}, f32[1,256]{1,0:T(1,128)}) custom-call(bf16[2,256,128]{2,1,0:T(8,128)(2,1)} %bitcast.3, bf16[4,12,256,256]{3,2,1,0:T(8,128)(2,1)} %tile_values.1, s32[4,12]{1,0:T(4,128)} %tile_row.1, s32[4,12]{1,0:T(4,128)} %tile_col.1, s32[4]{0:T(128)} %tile_count.1, bf16[128,256]{1,0:T(8,128)(2,1)} %weight.1, ...), custom_call_target="tpu_custom_call" | custom-call | tf_op jit(solution)/shard_map/pallas_call | solution.py:426
  46.8 13.1 %shard_map.104 = (bf16[512,256]{1,0:T(8,128)(2,1)}, f32[128,256]{1,0:T(8,128)}, f32[1,256]{1,0:T(1,128)}) custom-call(bf16[512,256]{1,0:T(8,128)(2,1)} %get-tuple-element.9.hidden, f32[128,256]{1,0:T(8,128)} %get-tuple-element.10.weight_grad, f32[1,256]{1,0:T(1,128)} %get-tuple-element.11.bias_grad), custom_call_target="tpu_custom_call" | custom-call | tf_op jit(solution)/shard_map/pallas_call | solution.py:486

commit v3 on v2

--- a/solution.py
+++ b/solution.py
@@ -74,6 +74,7 @@
     y_sem,
     xd_sem,
     yd_sem,
+    zd_sem,
     core_sem,
     pair_sem,
     rs_sem,
@@ -159,22 +160,30 @@
         def _():
             copy().start()
 
-    def diagonal(source):
+    def diagonal(source, crosses):
         mine, other = rows_of(source, b), rows_of(source, 1 - b)
         arrived(near.at[other], y_sem, source, y_dev)
-        second = 2 * (source * 2 + 1 - b) + 1
-        send(near.at[second], far.at[second], xd_sem, source, x_dev)
+        if crosses:
+            second = 2 * (source * 2 + 1 - b) + 1
+            send(near.at[second], far.at[second], xd_sem, source, x_dev)
         send(near.at[other], near_other.at[other], core_sem, n_z + source, c_dev)
         arrived(far.at[mine], x_sem, source, x_dev)
-        first = 2 * (source * 2 + b)
-        send(far.at[first], far.at[first], yd_sem, source, y_dev)
+        if crosses:
+            first = 2 * (source * 2 + b)
+            send(far.at[first], far.at[first], yd_sem, source, y_dev)
         send(far.at[mine], far_other.at[mine], core_sem, 2 * n_z + source, c_dev)
 
-    def last(source):
+    z_pair = (team, flip(z, 1) * 2 + b)
+
+    def last(source, crosses):
         other = rows_of(source, 1 - b)
         first = 2 * (source * 2 + 1 - b)
-        arrived(far.at[first + 1], xd_sem, source, x_dev)
-        arrived(far.at[first], yd_sem, source, y_dev)
+        if crosses:
+            arrived(far.at[first + 1], xd_sem, source, x_dev)
+            arrived(far.at[first], yd_sem, source, y_dev)
+            send(far.at[other], far.at[other], zd_sem, source, z_pair)
+        else:
+            arrived(far.at[other], zd_sem, source, z_pair)
         send(far.at[other], far_other.at[other], core_sem, 3 * n_z + source, c_dev)
 
     def both_ways(t, act):
@@ -210,9 +219,14 @@
             rows = rows_of(source, b)
             for sems in (y_sem, x_sem):
                 remote(near.at[rows], near.at[rows], sems, source, c_dev).wait_send()
-            for sems in (xd_sem, yd_sem):
+
+            @pl.when(lax.rem(z, 2) == source % 2)
+            def _():
                 one = near.at[2 * source]
-                remote(one, one, sems, source, c_dev).wait_send()
+                for sems in (xd_sem, yd_sem):
+                    remote(one, one, sems, source, c_dev).wait_send()
+                remote(near.at[rows], near.at[rows], zd_sem, source, c_dev).wait_send()
+
             for kind in range(4):
                 remote(near.at[rows], near.at[rows], core_sem, kind * n_z + source, c_dev).wait_send()
 
@@ -249,22 +263,29 @@
     total[...] = jnp.zeros_like(total)
     wg[...] = jnp.zeros_like(wg)
     bg[...] = jnp.zeros_like(bg)
+    def step_of(act, t):
+        if t == 0:
+            act(z, True)
+        else:
+            both_ways(t, lambda source, way: act(source, t % 2 == 0))
+
     for t in range(1, n_z):
         both_ways(t, receive)
         if t == 1:
-            diagonal(z)
-        else:
-            both_ways(t - 1, lambda source, way: diagonal(source))
-    both_ways(n_z - 1, lambda source, way: diagonal(source))
+            step_of(diagonal, 0)
+        if t % 2 == 0:
+            step_of(diagonal, t - 1)
+            step_of(last, t - 2)
+            step_of(diagonal, t)
+    step_of(last, n_z - 2)
+    step_of(diagonal, n_z - 1)
+    step_of(last, 1)
     aggregate(0, near)
-    last(z)
-    for t in range(1, n_z // 2):
-        both_ways(t, lambda source, way: last(source))
+    for t in range(3, n_z, 2):
+        step_of(last, t)
     from_core(near_other, 0, b)
     from_core(near_other, 1, 1 - b)
     aggregate(1, near_other)
-    for t in range(n_z // 2, n_z):
-        both_ways(t, lambda source, way: last(source))
     aggregate(2, far)
     from_core(far_other, 2, b)
     from_core(far_other, 3, 1 - b)
@@ -401,15 +422,16 @@
     store_hidden.wait()
 
 
-def hand_over(hidden, weight_grad, bias_grad, hidden_out, weight_out, bias_out, sems):
-    copies = [
-        pltpu.make_async_copy(hidden, hidden_out, sems.at[0]),
-        pltpu.make_async_copy(weight_grad, weight_out, sems.at[1]),
-        pltpu.make_async_copy(bias_grad, bias_out, sems.at[2]),
-    ]
-    for copy in copies:
+def hand_over(*refs):
+    ins, outs, held, load_sem, store_sem = refs[0:3], refs[3:6], refs[6:9], refs[9], refs[10]
+    loads = [pltpu.make_async_copy(ins[i], held[i], load_sem.at[i]) for i in range(3)]
+    stores = [pltpu.make_async_copy(held[i], outs[i], store_sem.at[i]) for i in range(3)]
+    for copy in loads:
         copy.start()
-    for copy in copies:
+    for load, store in zip(loads, stores):
+        load.wait()
+        store.start()
+    for copy in stores:
         copy.wait()
 
 
@@ -461,6 +483,7 @@
             dma((2, n_z)),
             dma((2, n_z)),
             dma((2, n_z)),
+            dma((2, n_z)),
             dma((2, 4 * n_z)),
             dma((2, 2)),
             dma((2, GROUP)),
@@ -488,7 +511,7 @@
         out_shape=shapes,
         in_specs=[anywhere] * 3,
         out_specs=[anywhere] * 3,
-        scratch_shapes=[dma((3,))],
+        scratch_shapes=[pltpu.VMEM(x.shape, x.dtype) for x in shapes] + [dma((3,)), dma((3,))],
         compiler_params=pltpu.CompilerParams(vmem_limit_bytes=60 * 1024 * 1024),
     )(hidden, weight_grad, bias_grad)
     return (hidden, weight_grad, bias_grad.reshape(wide))

time: 60 us -> 50.4 us (0.84)
  Pallas kernels: 59.2 us -> 49.6 us
    pallas_call x1, Pallas kernels: 13.1 us -> 1.75 us  [local(): pl.pallas_call(hand_over, out_shape=shapes, in_specs=[anywhere] * 3, out_...]
    pallas_call x1, Pallas kernels: 46.1 us -> 47.8 us  [local(): pl.pallas_call(functools.partial(kernel, n_row), out_shape=[jax.ShapeDtyp...]
where the time goes in v3:
time: 50.4 us; the launch traced here: 50.2 us
  Pallas kernels  49.6 us (98%)
  between operations  0.64 us (1%)
    pallas_call x1, Pallas kernels, local(): pl.pallas_call(functools.partial(kernel, n_row), out_shape=[jax.ShapeDtyp...  47.8 us
    pallas_call x1, Pallas kernels, local(): pl.pallas_call(hand_over, out_shape=shapes, in_specs=[anywhere] * 3, out_...  1.75 us

profile of v3, /device:TPU:0, one launch (start us, length us, event | category | flops | bytes accessed | tf_op | source)
XLA Modules:
  0.0 50.2 jit_solution(4190216414600395177)
XLA Ops:
  0.6 47.8 %shard_map.103 = (bf16[512,256]{1,0:T(8,128)(2,1)}, f32[128,256]{1,0:T(8,128)}, f32[1,256]{1,0:T(1,128)}) custom-call(bf16[2,256,128]{2,1,0:T(8,128)(2,1)} %bitcast.3, bf16[4,12,256,256]{3,2,1,0:T(8,128)(2,1)} %tile_values.1, s32[4,12]{1,0:T(4,128)} %tile_row.1, s32[4,12]{1,0:T(4,128)} %tile_col.1, s32[4]{0:T(128)} %tile_count.1, bf16[128,256]{1,0:T(8,128)(2,1)} %weight.1, ...), custom_call_target="tpu_custom_call" | custom-call | tf_op jit(solution)/shard_map/pallas_call | solution.py:448
  48.5 1.7 %shard_map.104 = (bf16[512,256]{1,0:T(8,128)(2,1)}, f32[128,256]{1,0:T(8,128)}, f32[1,256]{1,0:T(1,128)}) custom-call(bf16[512,256]{1,0:T(8,128)(2,1)} %get-tuple-element.9.refs_0_, f32[128,256]{1,0:T(8,128)} %get-tuple-element.10.refs_1_, f32[1,256]{1,0:T(1,128)} %get-tuple-element.11.refs_2_), custom_call_target="tpu_custom_call" | custom-call | tf_op jit(solution)/shard_map/pallas_call | solution.py:509

commit v4 on v2

--- a/solution.py
+++ b/solution.py
@@ -110,6 +110,10 @@
         for i, panel in enumerate(panels)
     ]
 
+    empty = 2 * n_row
+    for ref in (near, near_other, far, far_other):
+        ref[empty] = jnp.zeros((blk, LANES), jnp.bfloat16)
+
     barrier = pltpu.get_barrier_semaphore()
     greeted = [c_dev]
     for i in range(1, 2 * n_row):
@@ -117,8 +121,6 @@
         greeted.append((lax.div(flat, n_row) * 2 + core, lax.rem(flat, n_row)))
     for dev in greeted:
         pl.semaphore_signal(barrier, inc=1, device_id=dev, device_id_type=MESH)
-    for copy in tile_loads + loads:
-        copy.start()
     pl.semaphore_wait(barrier, len(greeted))
     load_own.wait()
 
@@ -226,12 +228,11 @@
             left, right = [], []
             for k in range(step):
                 s = base * step + k
-                block = feats[tile_col[panel, s]]
+                col = tile_col[panel, s]
                 live = s < count
                 place = tile_row[panel, s]
-                zero = jnp.zeros_like(block)
-                upper = jnp.where(live & (place == 0), block, zero)
-                lower = jnp.where(live & (place == 1), block, zero)
+                upper = feats[jnp.where(live & (place == 0), col, empty)]
+                lower = feats[jnp.where(live & (place == 1), col, empty)]
                 left.append(tiles[i, s])
                 right.append(jnp.concatenate([upper, lower], axis=1))
             total[...] += jnp.dot(
@@ -246,6 +247,8 @@
     pass_on(z, 0)
     pass_on(z, 1)
     full(z)
+    for copy in tile_loads + loads:
+        copy.start()
     total[...] = jnp.zeros_like(total)
     wg[...] = jnp.zeros_like(wg)
     bg[...] = jnp.zeros_like(bg)
@@ -311,9 +314,18 @@
         return (lax.div(member_now, 8) * 2 + core, group_now * 8 + lax.rem(member_now, 8))
 
     head = at(0, group)
-    for i in range(1, GROUP):
+    def loop(act):
+        def body(i, carry):
+            act(i)
+            return carry
+
+        lax.fori_loop(1, GROUP, body, 0)
+
+    def scatter(i):
         peer = lax.rem(member + i, GROUP)
-        sent.append(send(red.at[peer], scattered.at[member], rs_sem, i, at(peer, group)))
+        return remote(red.at[peer], scattered.at[member], rs_sem, i, at(peer, group))
+
+    loop(lambda i: scatter(i).start())
 
     @pl.when(member != 0)
     def _():
@@ -330,16 +342,17 @@
 
     scattered[member] = red[member]
     owned[1] = jnp.zeros((8, LANES), jnp.float32)
-    for i in range(1, GROUP):
+    def from_peer(ref, sems, i):
         peer = lax.rem(member + GROUP - i, GROUP)
-        arrived(scattered.at[peer], rs_sem, i, at(peer, group))
+        arrived(ref.at[peer], sems, i, at(peer, group))
+
+    loop(lambda i: from_peer(scattered, rs_sem, i))
     owned[0] = jnp.sum(scattered[...], axis=0)
 
     @pl.when(member == 0)
     def _():
         bias_in[0] = red[GROUP]
-        for i in range(1, GROUP):
-            remote(bias_in.at[i], bias_in.at[i], rb_sem, i, c_dev).wait_recv()
+        loop(lambda i: remote(bias_in.at[i], bias_in.at[i], rb_sem, i, c_dev).wait_recv())
         owned[1] = jnp.sum(bias_in[...], axis=0)
 
     n_group = n_row // 8
@@ -357,20 +370,20 @@
             ordered = ordered + crossed[lax.rem(group + n_group - g, n_group)]
         owned[...] = ordered
 
-    for i in range(1, GROUP):
+    def spread(i):
         peer = lax.rem(member + i, GROUP)
-        sent.append(send(owned.at[0], fin.at[member], ag_sem, i, at(peer, group)))
+        return remote(owned.at[0], fin.at[member], ag_sem, i, at(peer, group))
+
+    loop(lambda i: spread(i).start())
 
     @pl.when(member == 0)
     def _():
-        copies = [
-            remote(owned.at[1], fin.at[GROUP], ab_sem, i, at(i, group)) for i in range(1, GROUP)
-        ]
-        for copy in copies:
-            copy.start()
+        def spread_bias(i):
+            return remote(owned.at[1], fin.at[GROUP], ab_sem, i, at(i, group))
+
+        loop(lambda i: spread_bias(i).start())
         fin[GROUP] = owned[1]
-        for copy in copies:
-            copy.wait_send()
+        loop(lambda i: spread_bias(i).wait_send())
 
     @pl.when(member != 0)
     def _():
@@ -384,9 +397,7 @@
         ).wait_recv()
 
     fin[member] = owned[0]
-    for i in range(1, GROUP):
-        peer = lax.rem(member + GROUP - i, GROUP)
-        arrived(fin.at[peer], ag_sem, i, at(peer, group))
+    loop(lambda i: from_peer(fin, ag_sem, i))
     sent.append(send(fin, fin_other, pair_sem, 1, c_dev))
     arrived(fin_other, pair_sem, 1, c_dev)
     mine, other = fin[...], fin_other[...]
@@ -397,19 +408,22 @@
         bias_out[:, lanes] = half[GROUP, 0:1]
     for copy in sent:
         copy.wait_send()
+    loop(lambda i: scatter(i).wait_send())
+    loop(lambda i: spread(i).wait_send())
     all_sent()
     store_hidden.wait()
 
 
-def hand_over(hidden, weight_grad, bias_grad, hidden_out, weight_out, bias_out, sems):
-    copies = [
-        pltpu.make_async_copy(hidden, hidden_out, sems.at[0]),
-        pltpu.make_async_copy(weight_grad, weight_out, sems.at[1]),
-        pltpu.make_async_copy(bias_grad, bias_out, sems.at[2]),
-    ]
-    for copy in copies:
+def hand_over(*refs):
+    ins, outs, held, load_sem, store_sem = refs[0:3], refs[3:6], refs[6:9], refs[9], refs[10]
+    loads = [pltpu.make_async_copy(ins[i], held[i], load_sem.at[i]) for i in range(3)]
+    stores = [pltpu.make_async_copy(held[i], outs[i], store_sem.at[i]) for i in range(3)]
+    for copy in loads:
         copy.start()
-    for copy in copies:
+    for load, store in zip(loads, stores):
+        load.wait()
+        store.start()
+    for copy in stores:
         copy.wait()
 
 
@@ -433,10 +447,10 @@
         in_specs=[anywhere, anywhere, smem, smem, smem, anywhere, anywhere, anywhere],
         out_specs=[anywhere, vmem, vmem],
         scratch_shapes=[
-            pltpu.VMEM((2 * n_row, blk, width), jnp.bfloat16),
-            pltpu.VMEM((2 * n_row, blk, width), jnp.bfloat16),
-            pltpu.VMEM((2 * n_row, blk, width), jnp.bfloat16),
-            pltpu.VMEM((2 * n_row, blk, width), jnp.bfloat16),
+            pltpu.VMEM((2 * n_row + 1, blk, width), jnp.bfloat16),
+            pltpu.VMEM((2 * n_row + 1, blk, width), jnp.bfloat16),
+            pltpu.VMEM((2 * n_row + 1, blk, width), jnp.bfloat16),
+            pltpu.VMEM((2 * n_row + 1, blk, width), jnp.bfloat16),
             pltpu.VMEM((n_panel, slots, blk, blk), jnp.bfloat16),
             pltpu.VMEM((width, wide), jnp.bfloat16),
             pltpu.VMEM((1, wide), jnp.float32),
@@ -488,7 +502,7 @@
         out_shape=shapes,
         in_specs=[anywhere] * 3,
         out_specs=[anywhere] * 3,
-        scratch_shapes=[dma((3,))],
+        scratch_shapes=[pltpu.VMEM(x.shape, x.dtype) for x in shapes] + [dma((3,)), dma((3,))],
         compiler_params=pltpu.CompilerParams(vmem_limit_bytes=60 * 1024 * 1024),
     )(hidden, weight_grad, bias_grad)
     return (hidden, weight_grad, bias_grad.reshape(wide))

time: 60 us -> 48.9 us (0.81)
  Pallas kernels: 59.2 us -> 48.1 us
    pallas_call x1, Pallas kernels: 13.1 us -> 1.75 us  [local(): pl.pallas_call(hand_over, out_shape=shapes, in_specs=[anywhere] * 3, out_...]
where the time goes in v4:
time: 48.9 us; the launch traced here: 48.7 us
  Pallas kernels  48.1 us (98%)
  between operations  0.64 us (1%)
    pallas_call x1, Pallas kernels, local(): pl.pallas_call(functools.partial(kernel, n_row), out_shape=[jax.ShapeDtyp...  46.3 us
    pallas_call x1, Pallas kernels, local(): pl.pallas_call(hand_over, out_shape=shapes, in_specs=[anywhere] * 3, out_...  1.75 us

profile of v4, /device:TPU:0, one launch (start us, length us, event | category | flops | bytes accessed | tf_op | source)
XLA Modules:
  0.0 48.7 jit_solution(14248122006247304288)
XLA Ops:
  0.6 46.3 %shard_map.103 = (bf16[512,256]{1,0:T(8,128)(2,1)}, f32[128,256]{1,0:T(8,128)}, f32[1,256]{1,0:T(1,128)}) custom-call(bf16[2,256,128]{2,1,0:T(8,128)(2,1)} %bitcast.3, bf16[4,12,256,256]{3,2,1,0:T(8,128)(2,1)} %tile_values.1, s32[4,12]{1,0:T(4,128)} %tile_row.1, s32[4,12]{1,0:T(4,128)} %tile_col.1, s32[4]{0:T(128)} %tile_count.1, bf16[128,256]{1,0:T(8,128)(2,1)} %weight.1, ...), custom_call_target="tpu_custom_call" | custom-call | tf_op jit(solution)/shard_map/pallas_call | solution.py:440
  47.0 1.7 %shard_map.104 = (bf16[512,256]{1,0:T(8,128)(2,1)}, f32[128,256]{1,0:T(8,128)}, f32[1,256]{1,0:T(1,128)}) custom-call(bf16[512,256]{1,0:T(8,128)(2,1)} %get-tuple-element.9.refs_0_, f32[128,256]{1,0:T(8,128)} %get-tuple-element.10.refs_1_, f32[1,256]{1,0:T(1,128)} %get-tuple-element.11.refs_2_), custom_call_target="tpu_custom_call" | custom-call | tf_op jit(solution)/shard_map/pallas_call | solution.py:500

commit v5 on v4

--- a/solution.py
+++ b/solution.py
@@ -144,33 +144,39 @@
     def arrived(ref, sems, i, dev):
         remote(ref, ref, sems, i, dev).wait_recv()
 
-    def full(source):
-        rows = rows_of(source, b)
-        send(near.at[rows], near.at[rows], y_sem, source, y_dev)
-        send(near.at[rows], far.at[rows], x_sem, source, x_dev)
-        send(near.at[rows], near_other.at[rows], core_sem, source, c_dev)
-
-    def pass_on(source, way):
-        rows = rows_of(source, b)
+    def spot(source, b_now, h):
+        return 2 * (source * 2 + b_now) + h
+
+    def full(source, h):
+        one = near.at[spot(source, b, h)]
+        ways = [(y_sem, near, y_dev), (x_sem, far, x_dev)]
+        for sems, ref, dev in ways if h == 1 else ways[::-1]:
+            send(one, ref.at[spot(source, b, h)], sems, 2 * source + h, dev)
+
+    def to_core(ref, ref_other, kind, source, b_now):
+        rows = rows_of(source, b_now)
+        send(ref.at[rows], ref_other.at[rows], core_sem, kind * n_z + source, c_dev)
+
+    def pass_on(source, way, h):
+        one = near.at[spot(source, b, h)]
         dev = (team, (z + 1 - 2 * way) * 2 + b)
-
-        def copy():
-            return remote(near.at[rows], near.at[rows], z_sem, way * n_z + source, dev)
 
         @pl.when(z < n_z - 1 if way == 0 else z > 0)
         def _():
-            copy().start()
-
-    def diagonal(source):
-        mine, other = rows_of(source, b), rows_of(source, 1 - b)
-        arrived(near.at[other], y_sem, source, y_dev)
-        second = 2 * (source * 2 + 1 - b) + 1
+            remote(one, one, z_sem, 2 * (way * n_z + source) + h, dev).start()
+
+    def cross(source):
+        first, second = spot(source, b, 0), spot(source, 1 - b, 1)
+        arrived(far.at[first], x_sem, 2 * source, x_dev)
+        send(far.at[first], far.at[first], yd_sem, source, y_dev)
+        arrived(near.at[second], y_sem, 2 * source + 1, y_dev)
         send(near.at[second], far.at[second], xd_sem, source, x_dev)
-        send(near.at[other], near_other.at[other], core_sem, n_z + source, c_dev)
-        arrived(far.at[mine], x_sem, source, x_dev)
-        first = 2 * (source * 2 + b)
-        send(far.at[first], far.at[first], yd_sem, source, y_dev)
-        send(far.at[mine], far_other.at[mine], core_sem, 2 * n_z + source, c_dev)
+
+    def share(source):
+        arrived(near.at[spot(source, 1 - b, 0)], y_sem, 2 * source, y_dev)
+        to_core(near, near_other, 1, source, 1 - b)
+        arrived(far.at[spot(source, b, 1)], x_sem, 2 * source + 1, x_dev)
+        to_core(far, far_other, 2, source, b)
 
     def last(source):
         other = rows_of(source, 1 - b)
@@ -188,11 +194,12 @@
                 act(source, way)
 
     def receive(source, way):
-        rows = rows_of(source, b)
         dev = (team, (z - 1 + 2 * way) * 2 + b)
-        arrived(near.at[rows], z_sem, way * n_z + source, dev)
-        pass_on(source, way)
-        full(source)
+        for h in range(2):
+            arrived(near.at[spot(source, b, h)], z_sem, 2 * (way * n_z + source) + h, dev)
+            pass_on(source, way, h)
+            full(source, h)
+        to_core(near, near_other, 0, source, b)
 
     def from_core(ref, first, b_now):
         for j in range(n_z):
@@ -202,18 +209,21 @@
         for way in range(2):
             for source in range(n_z):
                 goes = (z < n_z - 1) & (z >= source) if way == 0 else (z > 0) & (z <= source)
-                rows = rows_of(source, b)
+                one = near.at[spot(source, b, 0)]
 
                 @pl.when(goes)
                 def _():
-                    remote(near.at[rows], near.at[rows], z_sem, way * n_z + source, c_dev).wait_send()
+                    for h in range(2):
+                        i = 2 * (way * n_z + source) + h
+                        remote(one, one, z_sem, i, c_dev).wait_send()
 
         for source in range(n_z):
             rows = rows_of(source, b)
+            one = near.at[spot(source, b, 0)]
             for sems in (y_sem, x_sem):
-                remote(near.at[rows], near.at[rows], sems, source, c_dev).wait_send()
+                for h in range(2):
+                    remote(one, one, sems, 2 * source + h, c_dev).wait_send()
             for sems in (xd_sem, yd_sem):
-                one = near.at[2 * source]
                 remote(one, one, sems, source, c_dev).wait_send()
             for kind in range(4):
                 remote(near.at[rows], near.at[rows], core_sem, kind * n_z + source, c_dev).wait_send()
@@ -244,21 +254,30 @@
 
         lax.fori_loop(0, slots // step, add, 0)
 
-    pass_on(z, 0)
-    pass_on(z, 1)
-    full(z)
+    for h in range(2):
+        pass_on(z, 0, h)
+        pass_on(z, 1, h)
+        full(z, h)
+    to_core(near, near_other, 0, z, b)
     for copy in tile_loads + loads:
         copy.start()
     total[...] = jnp.zeros_like(total)
     wg[...] = jnp.zeros_like(wg)
     bg[...] = jnp.zeros_like(bg)
+    def step_of(act, t):
+        if t == 0:
+            act(z)
+        else:
+            both_ways(t, lambda source, way: act(source))
+
     for t in range(1, n_z):
         both_ways(t, receive)
-        if t == 1:
-            diagonal(z)
-        else:
-            both_ways(t - 1, lambda source, way: diagonal(source))
-    both_ways(n_z - 1, lambda source, way: diagonal(source))
+        step_of(cross, t - 1)
+        if t > 1:
+            step_of(share, t - 2)
+    step_of(cross, n_z - 1)
+    step_of(share, n_z - 2)
+    step_of(share, n_z - 1)
     aggregate(0, near)
     last(z)
     for t in range(1, n_z // 2):
@@ -470,9 +489,9 @@
             pltpu.VMEM((1, wide), jnp.float32),
             dma((4,)),
             dma((4,)),
+            dma((2, 4 * n_z)),
             dma((2, 2 * n_z)),
-            dma((2, n_z)),
-            dma((2, n_z)),
+            dma((2, 2 * n_z)),
             dma((2, n_z)),
             dma((2, n_z)),
             dma((2, 4 * n_z)),

time: 48.9 us -> 47.9 us (0.980)
  Pallas kernels: 48.1 us -> 47 us
    pallas_call x1, Pallas kernels: 46.3 us -> 45.3 us  [local(): pl.pallas_call(functools.partial(kernel, n_row), out_shape=[jax.ShapeDtyp...]
where the time goes in v5:
time: 47.9 us; the launch traced here: 47.7 us
  Pallas kernels  47 us (98%)
  between operations  0.64 us (1%)
    pallas_call x1, Pallas kernels, local(): pl.pallas_call(functools.partial(kernel, n_row), out_shape=[jax.ShapeDtyp...  45.3 us
    pallas_call x1, Pallas kernels, local(): pl.pallas_call(hand_over, out_shape=shapes, in_specs=[anywhere] * 3, out_...  1.75 us

profile of v5, /device:TPU:0, one launch (start us, length us, event | category | flops | bytes accessed | tf_op | source)
XLA Modules:
  0.0 47.7 jit_solution(9648362584275361194)
XLA Ops:
  0.6 45.3 %shard_map.103 = (bf16[512,256]{1,0:T(8,128)(2,1)}, f32[128,256]{1,0:T(8,128)}, f32[1,256]{1,0:T(1,128)}) custom-call(bf16[2,256,128]{2,1,0:T(8,128)(2,1)} %bitcast.3, bf16[4,12,256,256]{3,2,1,0:T(8,128)(2,1)} %tile_values.1, s32[4,12]{1,0:T(4,128)} %tile_row.1, s32[4,12]{1,0:T(4,128)} %tile_col.1, s32[4]{0:T(128)} %tile_count.1, bf16[128,256]{1,0:T(8,128)(2,1)} %weight.1, ...), custom_call_target="tpu_custom_call" | custom-call | tf_op jit(solution)/shard_map/pallas_call | solution.py:459
  45.9 1.7 %shard_map.104 = (bf16[512,256]{1,0:T(8,128)(2,1)}, f32[128,256]{1,0:T(8,128)}, f32[1,256]{1,0:T(1,128)}) custom-call(bf16[512,256]{1,0:T(8,128)(2,1)} %get-tuple-element.9.refs_0_, f32[128,256]{1,0:T(8,128)} %get-tuple-element.10.refs_1_, f32[1,256]{1,0:T(1,128)} %get-tuple-element.11.refs_2_), custom_call_target="tpu_custom_call" | custom-call | tf_op jit(solution)/shard_map/pallas_call | solution.py:519

commit v6 on v5

--- a/solution.py
+++ b/solution.py
@@ -74,6 +74,7 @@
     y_sem,
     xd_sem,
     yd_sem,
+    zd_sem,
     core_sem,
     pair_sem,
     rs_sem,
@@ -165,12 +166,22 @@
         def _():
             remote(one, one, z_sem, 2 * (way * n_z + source) + h, dev).start()
 
+    z_paired = flip(z, 1)
+    pair_dev = (team, z_paired * 2 + b)
+
     def cross(source):
         first, second = spot(source, b, 0), spot(source, 1 - b, 1)
         arrived(far.at[first], x_sem, 2 * source, x_dev)
-        send(far.at[first], far.at[first], yd_sem, source, y_dev)
+
+        @pl.when(source != z_paired)
+        def _():
+            send(far.at[first], far.at[first], yd_sem, source, y_dev)
+
         arrived(near.at[second], y_sem, 2 * source + 1, y_dev)
-        send(near.at[second], far.at[second], xd_sem, source, x_dev)
+
+        @pl.when(source != z_paired)
+        def _():
+            send(near.at[second], far.at[second], xd_sem, source, x_dev)
 
     def share(source):
         arrived(near.at[spot(source, 1 - b, 0)], y_sem, 2 * source, y_dev)
@@ -180,10 +191,24 @@
 
     def last(source):
         other = rows_of(source, 1 - b)
-        first = 2 * (source * 2 + 1 - b)
-        arrived(far.at[first + 1], xd_sem, source, x_dev)
-        arrived(far.at[first], yd_sem, source, y_dev)
-        send(far.at[other], far_other.at[other], core_sem, 3 * n_z + source, c_dev)
+
+        @pl.when(source != z_paired)
+        def _():
+            arrived(far.at[spot(source, 1 - b, 1)], xd_sem, source, x_dev)
+            arrived(far.at[spot(source, 1 - b, 0)], yd_sem, source, y_dev)
+
+        @pl.when(source == z_paired)
+        def _():
+            arrived(far.at[other], zd_sem, 0, pair_dev)
+
+        to_core(far, far_other, 3, source, 1 - b)
+
+    def hand_own():
+        other = rows_of(z, 1 - b)
+        arrived(far.at[spot(z, 1 - b, 1)], xd_sem, z, x_dev)
+        arrived(far.at[spot(z, 1 - b, 0)], yd_sem, z, y_dev)
+        send(far.at[other], far.at[other], zd_sem, 0, pair_dev)
+        to_core(far, far_other, 3, z, 1 - b)
 
     def both_ways(t, act):
         for way in range(2):
@@ -206,6 +231,8 @@
             arrived(ref.at[rows_of(j, b_now)], core_sem, first * n_z + j, c_dev)
 
     def all_sent():
+        mine = rows_of(z, b)
+        remote(far.at[mine], far.at[mine], zd_sem, 0, c_dev).wait_send()
         for way in range(2):
             for source in range(n_z):
                 goes = (z < n_z - 1) & (z >= source) if way == 0 else (z > 0) & (z <= source)
@@ -223,8 +250,12 @@
             for sems in (y_sem, x_sem):
                 for h in range(2):
                     remote(one, one, sems, 2 * source + h, c_dev).wait_send()
-            for sems in (xd_sem, yd_sem):
-                remote(one, one, sems, source, c_dev).wait_send()
+
+            @pl.when(source != z_paired)
+            def _():
+                for sems in (xd_sem, yd_sem):
+                    remote(one, one, sems, source, c_dev).wait_send()
+
             for kind in range(4):
                 remote(near.at[rows], near.at[rows], core_sem, kind * n_z + source, c_dev).wait_send()
 
@@ -275,11 +306,12 @@
         step_of(cross, t - 1)
         if t > 1:
             step_of(share, t - 2)
+        if t == 2:
+            hand_own()
     step_of(cross, n_z - 1)
     step_of(share, n_z - 2)
     step_of(share, n_z - 1)
     aggregate(0, near)
-    last(z)
     for t in range(1, n_z // 2):
         both_ways(t, lambda source, way: last(source))
     from_core(near_other, 0, b)
@@ -494,6 +526,7 @@
             dma((2, 2 * n_z)),
             dma((2, n_z)),
             dma((2, n_z)),
+            dma((2, 1)),
             dma((2, 4 * n_z)),
             dma((2, 2)),
             dma((2, GROUP)),

time: 47.9 us -> 47 us (0.981)
  Pallas kernels: 47 us -> 46.2 us
    pallas_call x1, Pallas kernels: 45.3 us -> 44.4 us  [local(): pl.pallas_call(functools.partial(kernel, n_row), out_shape=[jax.ShapeDtyp...]
where the time goes in v6:
time: 47 us; the launch traced here: 46.8 us
  Pallas kernels  46.2 us (98%)
  between operations  0.64 us (1%)
    pallas_call x1, Pallas kernels, local(): pl.pallas_call(functools.partial(kernel, n_row), out_shape=[jax.ShapeDtyp...  44.4 us
    pallas_call x1, Pallas kernels, local(): pl.pallas_call(hand_over, out_shape=shapes, in_specs=[anywhere] * 3, out_...  1.75 us

profile of v6, /device:TPU:0, one launch (start us, length us, event | category | flops | bytes accessed | tf_op | source)
XLA Modules:
  0.0 46.8 jit_solution(1874155114986845034)
XLA Ops:
  0.6 44.4 %shard_map.103 = (bf16[512,256]{1,0:T(8,128)(2,1)}, f32[128,256]{1,0:T(8,128)}, f32[1,256]{1,0:T(1,128)}) custom-call(bf16[2,256,128]{2,1,0:T(8,128)(2,1)} %bitcast.3, bf16[4,12,256,256]{3,2,1,0:T(8,128)(2,1)} %tile_values.1, s32[4,12]{1,0:T(4,128)} %tile_row.1, s32[4,12]{1,0:T(4,128)} %tile_col.1, s32[4]{0:T(128)} %tile_count.1, bf16[128,256]{1,0:T(8,128)(2,1)} %weight.1, ...), custom_call_target="tpu_custom_call" | custom-call | tf_op jit(solution)/shard_map/pallas_call | solution.py:491
  45.1 1.7 %shard_map.104 = (bf16[512,256]{1,0:T(8,128)(2,1)}, f32[128,256]{1,0:T(8,128)}, f32[1,256]{1,0:T(1,128)}) custom-call(bf16[512,256]{1,0:T(8,128)(2,1)} %get-tuple-element.9.refs_0_, f32[128,256]{1,0:T(8,128)} %get-tuple-element.10.refs_1_, f32[1,256]{1,0:T(1,128)} %get-tuple-element.11.refs_2_), custom_call_target="tpu_custom_call" | custom-call | tf_op jit(solution)/shard_map/pallas_call | solution.py:552
